TPU v7x, 32 devices: a whole 2x2x4 slice. The times are simulated.
32 devices in a mesh: rows: 8 (over y, x, core), tiles: 4 (over z).
Axes of the slice: x: 2, y: 2, z: 4, core: 2. Of those that a mesh axis runs over, the one named last changes fastest.
Arguments:
- response_tiles: bfloat16 [8, 4, 15, 2, 256, 256], P('rows', 'tiles'), as said below
- tile_rows: int32 [8, 4, 15], P('rows', 'tiles'), may hold values from 0 to 2, as said below
- tile_cols: int32 [8, 4, 15], P('rows', 'tiles'), may hold values from 0 to 23, as said below
- tile_counts: int32 [8, 4], P('rows', 'tiles'), may hold values from 2 to 15, as said below
- start_block: bfloat16 [6144, 256], P(('rows', 'tiles')), may hold values from -6 to 6
Outputs:
- subspace: float32 [6144, 256], P(('rows', 'tiles'))
- rayleigh: float32 [2, 128, 128], replicated
Inputs may be any that keep to these rules, and one draw needn't show every extreme that they name: `tile_rows`: block rows within the group; every list's first two slots are live. `tile_cols`: A slot of group g at block row g * 3 + r has its column block within 3 of that block row, cut to the grid; in every list slot 0 lies 3 blocks below the row (or at column block 0) and slot 1 lies 3 blocks above it (or at the last column block). `tile_counts`: some tile list is full in every draw. `response_tiles`: real tiles of full rank; dead slots hold finite values.
All inputs are finite; a program needn't handle non-finite values.
Results may differ from a plain program's by a relative error of at most 0.0038.
Values may be sent and summed in bfloat16 or wider, within the bound.
A program may use at most 64 MiB of HBM per device.

v0:
```python
import math

import jax
import jax.numpy as jnp
import numpy as np
from jax import lax
from jax.sharding import PartitionSpec as P

ITERS = 2


HIGH = lax.Precision.HIGHEST


def with_halo(block, sides, width):
    for axis, dim in sides:
        count = lax.axis_size(axis)
        forward = [(i, i + 1) for i in range(count - 1)]
        backward = [(target, source) for source, target in forward]
        low = lax.ppermute(
            lax.slice_in_dim(block, block.shape[dim] - width, None, axis=dim), axis, forward
        )
        high = lax.ppermute(lax.slice_in_dim(block, 0, width, axis=dim), axis, backward)
        block = jnp.concatenate([low, block, high], axis=dim)
    return block


def passed_along(value, axis, steps):
    count = lax.axis_size(axis)
    leading, last = (max(0, -steps), min(count, count - steps))
    return lax.ppermute(value, axis, [(source, source + steps) for source in range(leading, last)])


def inner(left_side, right_side):
    return lax.dot_general(left_side, right_side, (((0,), (0,)), ((), ())), precision=HIGH)


def whitening(gram, columns, nodes):
    upper_left = gram[:columns, :columns]
    upper_right = gram[:columns, columns:]
    lower_left = gram[columns:, :columns]
    lower_right = gram[columns:, columns:]
    real_gram = upper_left + lower_right
    imag_gram = upper_right - lower_left
    embedded = jnp.concatenate(
        [jnp.concatenate([real_gram, imag_gram], 1), jnp.concatenate([-imag_gram, real_gram], 1)], 0
    )
    pairing = np.stack([np.arange(columns), np.arange(columns) + columns], 1).reshape(-1)
    unpairing = np.argsort(pairing)
    paired = embedded[pairing][:, pairing]
    factor = jnp.linalg.cholesky(paired)
    identity = jnp.eye(2 * columns, dtype=gram.dtype)
    inverse = jax.scipy.linalg.solve_triangular(factor, identity, lower=True)
    return inverse.T[unpairing][:, unpairing] * math.sqrt(nodes)


def rayleigh_of(products, columns, nodes):
    real_part = products[:columns, :columns] + products[columns:, columns:]
    imag_part = products[:columns, columns:] - products[columns:, :columns]
    return jnp.stack([real_part, imag_part]) / nodes


def forward_tiles(slots, row_list, col_list, live_count, extended, first_block, own_rows):
    tile_size = slots.shape[-1]
    width = extended.shape[1]
    half = width // 2

    def forward_visit(slot_index, totals):
        pair = lax.dynamic_index_in_dim(slots, slot_index, 0, keepdims=False)
        source = lax.dynamic_slice_in_dim(
            extended, (col_list[slot_index] - first_block) * tile_size, tile_size, 0
        )
        real_term = jnp.dot(pair[0], source, preferred_element_type=jnp.float32)
        imag_term = jnp.dot(pair[1], source, preferred_element_type=jnp.float32)
        term = jnp.concatenate(
            [real_term[:, :half] - imag_term[:, half:], real_term[:, half:] + imag_term[:, :half]],
            1,
        )
        target = row_list[slot_index] * tile_size
        present = lax.dynamic_slice_in_dim(totals, target, tile_size, 0)
        return lax.dynamic_update_slice_in_dim(totals, present + term, target, 0)

    return lax.fori_loop(0, live_count, forward_visit, jnp.zeros((own_rows, width), jnp.float32))


def adjoint_tiles(slots, row_list, col_list, live_count, narrow, first_block, own_rows):
    tile_size = slots.shape[-1]
    width = narrow.shape[1]
    half = width // 2
    contract = (((0,), (0,)), ((), ()))

    def adjoint_visit(slot_index, totals):
        pair = lax.dynamic_index_in_dim(slots, slot_index, 0, keepdims=False)
        source = lax.dynamic_slice_in_dim(narrow, row_list[slot_index] * tile_size, tile_size, 0)
        real_term = lax.dot_general(pair[0], source, contract, preferred_element_type=jnp.float32)
        imag_term = lax.dot_general(pair[1], source, contract, preferred_element_type=jnp.float32)
        term = jnp.concatenate(
            [real_term[:, :half] + imag_term[:, half:], real_term[:, half:] - imag_term[:, :half]],
            1,
        )
        target = (col_list[slot_index] - first_block) * tile_size
        present = lax.dynamic_slice_in_dim(totals, target, tile_size, 0)
        return lax.dynamic_update_slice_in_dim(totals, present + term, target, 0)

    return lax.fori_loop(
        0, live_count, adjoint_visit, jnp.zeros((3 * own_rows, width), jnp.float32)
    )


def on_device(response_tiles, tile_rows, tile_cols, tile_counts, start_block):
    slots = response_tiles[0, 0]
    row_list = tile_rows[0, 0]
    col_list = tile_cols[0, 0]
    live_count = tile_counts[0, 0]
    tile_size = slots.shape[-1]
    shard_rows = start_block.shape[0]
    width = start_block.shape[1]
    columns = width // 2
    own_rows = shard_rows * lax.axis_size("tiles")
    blocks = own_rows // tile_size
    first_block = lax.axis_index("rows") * blocks - blocks
    nodes = own_rows * lax.axis_size("rows")
    current = start_block.astype(jnp.float32)
    rayleigh = jnp.zeros((2, columns, columns), jnp.float32)
    for iteration in range(ITERS):
        is_last = iteration == ITERS - 1
        narrow = current.astype(jnp.bfloat16)
        gathered = lax.all_gather(narrow, "tiles", axis=0, tiled=True)
        extended = with_halo(gathered, (("rows", 0),), own_rows)
        response = forward_tiles(
            slots, row_list, col_list, live_count, extended, first_block, own_rows
        )
        summed = lax.psum(response, "tiles")
        response_narrow = summed.astype(jnp.bfloat16)
        spread = adjoint_tiles(
            slots, row_list, col_list, live_count, response_narrow, first_block, own_rows
        )
        lower_rim = spread[:own_rows]
        middle = spread[own_rows : 2 * own_rows]
        upper_rim = spread[2 * own_rows :]
        from_below = passed_along(upper_rim, "rows", 1)
        from_above = passed_along(lower_rim, "rows", -1)
        adjoint_rows = lax.psum_scatter(
            middle + from_below + from_above, "tiles", scatter_dimension=0, tiled=True
        )
        image = adjoint_rows + current
        gram_term = inner(image, image)
        if is_last:
            gram, products = lax.psum((gram_term, inner(current, image)), ("rows", "tiles"))
            rayleigh = rayleigh_of(products, columns, nodes)
        else:
            gram = lax.psum(gram_term, ("rows", "tiles"))
        current = jnp.dot(image, whitening(gram, columns, nodes), precision=HIGH)
    return (current, rayleigh)


def solution(mesh):
    in_specs = (
        P("rows", "tiles", None, None, None, None),
        P("rows", "tiles", None),
        P("rows", "tiles", None),
        P("rows", "tiles"),
        P(("rows", "tiles"), None),
    )
    out_specs = (P(("rows", "tiles"), None), P())
    return jax.shard_map(
        on_device, mesh=mesh, in_specs=in_specs, out_specs=out_specs, check_vma=False
    )
```

profile of v0, /device:TPU:11, one launch (start us, length us, event | category | flops | bytes accessed | tf_op | source)
XLA Modules:
  0.0 955.1 jit_solution(14878841919763353992)
XLA Ops:
  7.2 12.0 %all_gather.6 = bf16[768,256]{1,0:T(8,128)(2,1)S(1)} all-gather(bf16[192,256]{1,0:T(8,128)(2,1)} %param.32), channel_id=1, replica_groups=mesh['rows'=8,'tiles'=4] {'tiles'}, dimensions={0}, use_global_device_ids=true | all-gather | bytes 491520 | tf_op jit(solution)/shard_map/all_gather | solution.py:128
  19.2 7.3 collective-permute-start
  28.4 4.2 collective-permute-done
  32.6 4.5 collective-permute-done.1
  37.2 53.3 %while.44 = (s32[]{:T(128)}, f32[768,256]{1,0:T(8,128)S(1)}, s32[]{:T(128)}, s32[15]{0:T(128)S(1)}, bf16[15,2,256,256]{3,2,1,0:T(8,128)(2,1)}, /*index=5*/s32[15...) while((s32[]{:T(128)}, f32[768,256]{1,0:T(8,128)S(1)}, ...), condition=%wide.region_1.2_spmd, body=%wide.region_0.1_spmd.sunk | while | flops 67305488 | bytes 4718943 | solution.py:83
  90.6 54.9 %all-reduce.10 = bf16[768,256]{1,0:T(8,128)(2,1)S(1)} all-reduce(f32[768,256]{1,0:T(8,128)S(1)} %get-tuple-element.176), channel_id=1, replica_groups=mesh['rows'=8,'tiles'=4] {'tiles'}, use_global_device_ids=true, to_apply=%region_2.3 | all-reduce | flops 196608 | bytes 1179648 | tf_op jit(solution)/shard_map/psum | solution.py:133
  145.6 50.6 %while.45 = (s32[]{:T(128)}, f32[2304,256]{0,1:T(8,128)S(1)}, s32[]{:T(128)}, s32[15]{0:T(128)S(1)}, s32[]{:T(128)}, /*index=5*/bf16[15,2,256,256]{3,2,1,0:T(8,1...) while((s32[]{:T(128)}, f32[2304,256]{0,1:T(8,128)S(1)}, ...), condition=%wide.region_4.5_spmd, body=%wide.region_3.4_spmd.sunk | while | flops 67305488 | bytes 2621787 | solution.py:105
  198.2 2.5 collective-permute-start.3
  200.8 11.9 %collective-permute-done.2 = f32[768,256]{0,1:T(8,128)S(1)} collective-permute-done((f32[768,256]{0,1:T(8,128)S(1)}, f32[768,256]{0,1:T(8,128)S(1)}, u32[]{:S(2)}, u32[]{:S(2)}) %collective-permute-start.2) | collective-permute-done | bytes 786464 | tf_op jit(solution)/shard_map/ppermute | solution.py:31
  214.2 56.9 %reduce-scatter.7.cloned.1.call-done = f32[192,256]{1,0:T(8,128)} async-done(((f32[768,256]{1,0:T(8,128)}), f32[192,256]{1,0:T(8,128)}) %reduce-scatter.7.cloned.1.call-update) | async-done | bytes 196624
  273.9 127.1 %all-reduce.7.cloned.1.call-done = f32[256,256]{1,0:T(8,128)} async-done(((f32[256,256]{1,0:T(8,128)}), f32[256,256]{1,0:T(8,128)}) %all-reduce.7.cloned.1.call-update) | async-done | bytes 262160 | tf_op jit(solution)/shard_map/psum | solution.py:152
  404.3 11.7 %cholesky.130 = f32[128,128]{1,0:T(8,128)S(1)} custom-call(f32[128,128]{1,0:T(8,128)S(1)} %cholesky.194), custom_call_target="Cholesky" | custom-call | tf_op jit(solution)/shard_map/jit(cholesky)/cholesky | solution.py:51
  416.0 9.8 %custom-call.13 = f32[1,128,128]{1,2,0:T(8,128)S(1)} custom-call(f32[1,128,128]{2,1,0:T(8,128)S(1)} %get-tuple-element.309), custom_call_target="InvertDiagBlocksLowerTriangular" | custom-call | tf_op jit(solution)/shard_map/jit(cholesky)/cholesky | solution.py:51
  426.3 11.7 %cholesky.147 = f32[128,128]{1,0:T(8,128)S(1)} custom-call(f32[128,128]{1,0:T(8,128)S(1)} %convolution_subtract_fusion.3), custom_call_target="Cholesky" | custom-call | tf_op jit(solution)/shard_map/jit(cholesky)/cholesky | solution.py:51
  440.1 4.1 while.48
  444.8 19.7 %custom-call.14 = f32[2,128,128]{1,2,0:T(8,128)S(1)} custom-call(f32[2,128,128]{2,1,0:T(8,128)S(1)} %get-tuple-element.194), custom_call_target="InvertDiagBlocksLowerTriangular" | custom-call | tf_op jit(solution)/shard_map/jit(_solve_triangular)/triangular_solve | solution.py:53
  468.9 12.4 %all_gather.7 = bf16[768,256]{1,0:T(8,128)(2,1)S(1)} all-gather(bf16[192,256]{1,0:T(8,128)(2,1)S(1)} %get-tuple-element.312), channel_id=1, replica_groups=mesh['rows'=8,'tiles'=4] {'tiles'}, dimensions={0}, use_global_device_ids=true | all-gather | bytes 491520 | tf_op jit(solution)/shard_map/all_gather | solution.py:128
  481.3 7.4 collective-permute-start.4
  490.7 4.2 collective-permute-done.4
  494.8 3.9 collective-permute-done.5
  498.9 55.2 %while.46 = (s32[]{:T(128)}, f32[768,256]{1,0:T(8,128)S(1)}, s32[]{:T(128)}, s32[15]{0:T(128)S(1)}, bf16[15,2,256,256]{3,2,1,0:T(8,128)(2,1)}, /*index=5*/s32[15...) while((s32[]{:T(128)}, f32[768,256]{1,0:T(8,128)S(1)}, ...), condition=%wide.region_12.15_spmd, body=%wide.region_11.14_spmd.sunk | while | flops 67305488 | bytes 4718943 | solution.py:83
  554.1 58.5 %all-reduce.11 = bf16[768,256]{1,0:T(8,128)(2,1)S(1)} all-reduce(f32[768,256]{1,0:T(8,128)S(1)} %get-tuple-element.178), channel_id=1, replica_groups=mesh['rows'=8,'tiles'=4] {'tiles'}, use_global_device_ids=true, to_apply=%region_13.16 | all-reduce | flops 196608 | bytes 1179648 | tf_op jit(solution)/shard_map/psum | solution.py:133
  612.8 55.2 %while.47 = (s32[]{:T(128)}, f32[2304,256]{1,0:T(8,128)S(1)}, s32[]{:T(128)}, s32[15]{0:T(128)S(1)}, s32[]{:T(128)}, /*index=5*/bf16[15,2,256,256]{3,2,1,0:T(8,1...) while((s32[]{:T(128)}, f32[2304,256]{1,0:T(8,128)S(1)}, ...), condition=%wide.region_15.18_spmd, body=%wide.region_14.17_spmd.sunk | while | flops 67305488 | bytes 4718943 | solution.py:105
  670.1 2.4 collective-permute-start.7
  672.6 12.2 %collective-permute-done.6 = f32[768,256]{1,0:T(8,128)S(1)} collective-permute-done((f32[768,256]{1,0:T(8,128)S(1)}, f32[768,256]{1,0:T(8,128)S(1)}, u32[]{:S(2)}, u32[]{:S(2)}) %collective-permute-start.6) | collective-permute-done | bytes 786464 | tf_op jit(solution)/shard_map/ppermute | solution.py:31
  686.2 59.7 %reduce-scatter.5.cloned.1.call-done = f32[192,256]{1,0:T(8,128)} async-done(((f32[768,256]{1,0:T(8,128)}), f32[192,256]{1,0:T(8,128)}) %reduce-scatter.5.cloned.1.call-update) | async-done | bytes 196624 | tf_op jit(solution)/shard_map/reduce_scatter | solution.py:143
  749.6 129.2 %all-reduce.9.cloned.1.call-done = (f32[256,256]{1,0:T(8,128)}, f32[256,256]{1,0:T(8,128)}) async-done(((f32[256,256]{1,0:T(8,128)}, f32[256,256]{1,0:T(8,128)}), (f32[256,256]{1,0:T(8,128)}, f32[256,256]{1,0:T(8,128)})) %all-reduce.9.cloned.1.call-update) | async-done | bytes 524304 | tf_op jit(solution)/shard_map/psum | solution.py:149
  883.0 11.7 %cholesky.164 = f32[128,128]{1,0:T(8,128)S(1)} custom-call(f32[128,128]{1,0:T(8,128)S(1)} %cholesky.197), custom_call_target="Cholesky" | custom-call | tf_op jit(solution)/shard_map/jit(cholesky)/cholesky | solution.py:51
  894.7 9.8 %custom-call.15 = f32[1,128,128]{1,2,0:T(8,128)S(1)} custom-call(f32[1,128,128]{2,1,0:T(8,128)S(1)} %get-tuple-element.305), custom_call_target="InvertDiagBlocksLowerTriangular" | custom-call | tf_op jit(solution)/shard_map/jit(cholesky)/cholesky | solution.py:51
  905.0 11.9 %cholesky.181 = f32[128,128]{1,0:T(8,128)S(1)} custom-call(f32[128,128]{1,0:T(8,128)S(1)} %convolution_subtract_fusion.2), custom_call_target="Cholesky" | custom-call | tf_op jit(solution)/shard_map/jit(cholesky)/cholesky | solution.py:51
  919.7 4.0 while.49
  923.7 19.7 %custom-call.16 = f32[2,128,128]{1,2,0:T(8,128)S(1)} custom-call(f32[2,128,128]{2,1,0:T(8,128)S(1)} %get-tuple-element.195), custom_call_target="InvertDiagBlocksLowerTriangular" | custom-call | tf_op jit(solution)/shard_map/jit(_solve_triangular)/triangular_solve | solution.py:53
  (445 shorter events, 184.2 us)
Async XLA Ops:
  7.2 30.0 %copy-start.6 = (s32[1,1,15]{2,1,0:T(1,128)S(1)}, s32[1,1,15]{2,1,0:T(1,128)}, u32[]{:S(2)}) copy-start(s32[1,1,15]{2,1,0:T(1,128)} %param.30) | copy-start | bytes 184
  7.2 30.0 %copy-start.7 = (s32[1,1,15]{2,1,0:T(1,128)S(1)}, s32[1,1,15]{2,1,0:T(1,128)}, u32[]{:S(2)}) copy-start(s32[1,1,15]{2,1,0:T(1,128)} %param.29) | copy-start | bytes 184
  7.2 263.9 %reduce-scatter.7.cloned.1.call-start = ((), (), s32[]{:S(2)}) async-start(), calls=%async_computation.4 | async-start | bytes 983040
  19.2 13.4 %collective-permute-start = (bf16[768,256]{1,0:T(8,128)(2,1)S(1)}, bf16[768,256]{1,0:T(8,128)(2,1)S(1)}, u32[]{:S(2)}, u32[]{:S(2)}) collective-permute-start(bf16[768,256]{1,0:T(8,128)(2,1)S(1)} %all_gather.6), channel_id=1, source_target_pairs={{0,4},{4,8},{8,12},{12,16},{16,20},{20,24},{24,28},{1,5},{5,9},{9,... | collective-permute-start | bytes 1179656 | tf_op jit(solution)/shard_map/ppermute | solution.py:20
  26.5 10.6 %collective-permute-start.1 = (bf16[768,256]{1,0:T(8,128)(2,1)S(1)}, bf16[768,256]{1,0:T(8,128)(2,1)S(1)}, u32[]{:S(2)}, u32[]{:S(2)}) collective-permute-start(bf16[768,256]{1,0:T(8,128)(2,1)S(1)} %all_gather.6), channel_id=1, source_target_pairs={{4,0},{8,4},{12,8},{16,12},{20,16},{24,20},{28,24},{5,1},{9,5},{13... | collective-permute-start | bytes 1179656 | tf_op jit(solution)/shard_map/ppermute | solution.py:23
  196.3 16.4 %collective-permute-start.2 = (f32[768,256]{0,1:T(8,128)S(1)}, f32[768,256]{0,1:T(8,128)S(1)}, u32[]{:S(2)}, u32[]{:S(2)}) collective-permute-start(f32[768,256]{0,1:T(8,128)S(1)} %get-tuple-element.296), channel_id=1, source_target_pairs={{0,4},{4,8},{8,12},{12,16},{16,20},{20,24},{24,28},{1,5},{5,9},{9,... | collective-permute-start | bytes 2359304 | tf_op jit(solution)/shard_map/ppermute | solution.py:31
  198.2 15.9 %copy-start.3 = (bf16[192,256]{1,0:T(8,128)(2,1)S(1)}, bf16[192,256]{1,0:T(8,128)(2,1)}, u32[]{:S(2)}) copy-start(bf16[192,256]{1,0:T(8,128)(2,1)} %param.32) | copy-start | bytes 294916
  198.2 16.0 %copy-start.5 = (s32[256]{0:T(256)S(1)}, s32[256]{0:T(256)}, u32[]{:S(2)}) copy-start(s32[256]{0:T(256)} %constant.181) | copy-start | bytes 3076
  198.2 16.0 %copy-start.4 = (s32[256]{0:T(256)S(1)}, s32[256]{0:T(256)}, u32[]{:S(2)}) copy-start(s32[256]{0:T(256)} %constant.183) | copy-start | bytes 3076
  198.2 14.5 %collective-permute-start.3 = (f32[768,256]{0,1:T(8,128)S(1)}, f32[768,256]{0,1:T(8,128)S(1)}, u32[]{:S(2)}, u32[]{:S(2)}) collective-permute-start(f32[768,256]{0,1:T(8,128)S(1)} %get-tuple-element.297), channel_id=1, source_target_pairs={{4,0},{8,4},{12,8},{16,12},{20,16},{24,20},{28,24},{5,1},{9,5},{13... | collective-permute-start | bytes 2359304 | tf_op jit(solution)/shard_map/ppermute | solution.py:31
  214.0 187.0 %all-reduce.7.cloned.1.call-start = ((), (), s32[]{:S(2)}) async-start(), calls=%async_computation.2 | async-start | bytes 524288 | tf_op jit(solution)/shard_map/psum | solution.py:152
  273.3 472.5 %reduce-scatter.5.cloned.1.call-start = ((), (), s32[]{:S(2)}) async-start(), calls=%async_computation.3 | async-start | bytes 983040 | tf_op jit(solution)/shard_map/reduce_scatter | solution.py:143
  273.9 190.9 %copy-start = (f32[256,256]{1,0:T(8,128)}, f32[256,256]{1,0:T(8,128)S(1)}, u32[]{:S(2)}) copy-start(f32[256,256]{1,0:T(8,128)S(1)} %fusion.29) | copy-start | bytes 786436
  444.3 0.6 copy-start.8
  481.3 13.5 %collective-permute-start.4 = (bf16[768,256]{1,0:T(8,128)(2,1)S(1)}, bf16[768,256]{1,0:T(8,128)(2,1)S(1)}, u32[]{:S(2)}, u32[]{:S(2)}) collective-permute-start(bf16[768,256]{1,0:T(8,128)(2,1)S(1)} %all_gather.7), channel_id=1, source_target_pairs={{0,4},{4,8},{8,12},{12,16},{16,20},{20,24},{24,28},{1,5},{5,9},{9,... | collective-permute-start | bytes 1179656 | tf_op jit(solution)/shard_map/ppermute | solution.py:20
  488.7 10.0 %collective-permute-start.5 = (bf16[768,256]{1,0:T(8,128)(2,1)S(1)}, bf16[768,256]{1,0:T(8,128)(2,1)S(1)}, u32[]{:S(2)}, u32[]{:S(2)}) collective-permute-start(bf16[768,256]{1,0:T(8,128)(2,1)S(1)} %all_gather.7), channel_id=1, source_target_pairs={{4,0},{8,4},{12,8},{16,12},{20,16},{24,20},{28,24},{5,1},{9,5},{13... | collective-permute-start | bytes 1179656 | tf_op jit(solution)/shard_map/ppermute | solution.py:23
  668.1 77.8 %copy-start.2 = (f32[192,256]{1,0:T(8,128)S(1)}, f32[192,256]{1,0:T(8,128)}, u32[]{:S(2)}) copy-start(f32[192,256]{1,0:T(8,128)} %get-tuple-element.313) | copy-start | bytes 589828
  668.1 16.7 %collective-permute-start.6 = (f32[768,256]{1,0:T(8,128)S(1)}, f32[768,256]{1,0:T(8,128)S(1)}, u32[]{:S(2)}, u32[]{:S(2)}) collective-permute-start(f32[768,256]{1,0:T(8,128)S(1)} %get-tuple-element.294), channel_id=1, source_target_pairs={{0,4},{4,8},{8,12},{12,16},{16,20},{20,24},{24,28},{1,5},{5,9},{9,... | collective-permute-start | bytes 2359304 | tf_op jit(solution)/shard_map/ppermute | solution.py:31
  670.1 14.7 %collective-permute-start.7 = (f32[768,256]{1,0:T(8,128)S(1)}, f32[768,256]{1,0:T(8,128)S(1)}, u32[]{:S(2)}, u32[]{:S(2)}) collective-permute-start(f32[768,256]{1,0:T(8,128)S(1)} %get-tuple-element.295), channel_id=1, source_target_pairs={{4,0},{8,4},{12,8},{16,12},{20,16},{24,20},{28,24},{5,1},{9,5},{13... | collective-permute-start | bytes 2359304 | tf_op jit(solution)/shard_map/ppermute | solution.py:31
  685.9 192.8 %all-reduce.9.cloned.1.call-start = ((), (), s32[]{:S(2)}) async-start(), calls=%async_computation.5 | async-start | bytes 1048576 | tf_op jit(solution)/shard_map/psum | solution.py:149
  881.8 37.9 %copy-start.9 = (s32[2,2]{1,0:T(2,128)S(1)}, s32[2,2]{1,0:T(2,128)}, u32[]{:S(2)}) copy-start(s32[2,2]{1,0:T(2,128)} %copy-done.8) | copy-start | bytes 52
  882.8 60.6 %copy-start.1 = (f32[256,256]{1,0:T(8,128)S(1)}, f32[256,256]{1,0:T(8,128)}, u32[]{:S(2)}) copy-start(f32[256,256]{1,0:T(8,128)} %copy-done) | copy-start | bytes 786436
Sparse Core Ops, SparseCore 0:
  214.2 56.9 reduce-scatter.6
  276.6 124.3 all-reduce.6
  686.0 59.7 reduce-scatter.4
  751.1 127.5 all-reduce.8
where the time goes:
time: 963 us; the launch traced here: 955 us
  waiting for transfers between devices  414 us (43%)
  blocking collectives  138 us (14%)
  other arithmetic  117 us (12%)
  matrix products  91 us (9%)
  loops' own time  76.6 us (8%)
  local copies, waits for them, and re-layouts  73.6 us (8%)
  starting transfers between devices  28.4 us (3%)
  between operations  17.3 us (2%)
    psum x1, waiting for transfers between devices, on_device(): lax.psum((gram_term, inner(current, image)), ('rows', 'tiles'))  129 us
    psum x1, waiting for transfers between devices, on_device(): gram = lax.psum(gram_term, ('rows', 'tiles'))  127 us
    psum x2, blocking collectives, on_device(): summed = lax.psum(response, 'tiles')  113 us
    another operation x13, other arithmetic, whitening(): factor = jnp.linalg.cholesky(paired)  68.8 us
    reduce_scatter x1, waiting for transfers between devices, on_device(): lax.psum_scatter(middle + from_below + from_above, 'tiles', scatter_dimen...  59.7 us
    unnamed x5, waiting for transfers between devices  56.9 us
    another operation x5, other arithmetic, whitening(): inverse = jax.scipy.linalg.solve_triangular(factor, identity, lower=True)  39.4 us
    another operation x2, loops' own time, adjoint_tiles(): lax.fori_loop(0, live_count, adjoint_visit, jnp.zeros((3 * own_rows, widt...  38.2 us
  transfers between devices with their start and end apart: 12, of which 10 were waited for; matrix products, arithmetic and copies ran while one was open for 0% of the time, Pallas kernels for 0%

commit v1 on v0

v1 whole, which is shorter than its diff:
```python
import functools
import math

import jax
import jax.numpy as jnp
from jax import lax
from jax.experimental import pallas as pl
from jax.experimental.pallas import tpu as pltpu
from jax.sharding import PartitionSpec as P

HIGH = lax.Precision.HIGHEST
MESH = pl.DeviceIdType.MESH
VMEM_BYTES = 48 * 1024 * 1024
F32 = jnp.float32
BF16 = jnp.bfloat16


def ordered(key, other, outs):
    count = key.shape[0]
    slot = jnp.arange(count, dtype=jnp.int32)
    before = (key[:, None] < key[None, :]) | (
        (key[:, None] == key[None, :]) & (slot[:, None] < slot[None, :])
    )
    rank = jnp.sum(before.astype(jnp.int32), 0)
    hot = (rank[:, None] == slot[None, :]).astype(jnp.int32)
    order = jnp.sum(hot * slot[:, None], 0)
    target = jnp.sum(hot * key[:, None], 0)
    source = jnp.sum(hot * other[:, None], 0)
    same = jnp.concatenate([jnp.zeros((1,), bool), target[1:] == target[:-1]])
    previous = jnp.where(same, slot, 0)
    out = jnp.arange(outs, dtype=jnp.int32)
    upto = jnp.sum((target[:, None] <= out[None, :]).astype(jnp.int32), 0)
    present = jnp.any(target[:, None] == out[None, :], 0)
    return jnp.concatenate([order, source, previous, jnp.where(present, upto, 0)])


def step_kernel(
    n_g, n_t, with_products, slots_n, blocks,
    plan, tiles, current, image_out, gram_out,
    turned, ext, ext_blocks, z_blocks, runs, part32, part, rs_in, z_rows, spread, mid, halo_in, ar_out, ar_in,
    gram_mine, gram_in, gram_rows, gram_sum,
    gz_s, gz_r, gh_s, gh_r, rs_s, rs_r, ag_s, ag_r, ah_s, ah_r, ar_s, ar_r,
    g1_s, g1_r, g2_s, g2_r, g3_s, g3_r,
):
    g = lax.axis_index("rows")
    t = lax.axis_index("tiles")
    has_low = g > 0
    has_high = g < n_g - 1
    tile = tiles.shape[-1]
    shard, width = current.shape
    half = width // 2
    own = shard * n_t

    barrier = pltpu.get_barrier_semaphore()
    for k in range(1, n_t):
        pl.semaphore_signal(barrier, inc=1, device_id=(g, (t + k) % n_t), device_id_type=MESH)

    for k in range(1, n_g):
        pl.semaphore_signal(barrier, inc=1, device_id=((g + k) % n_g, t), device_id_type=MESH)
    pl.semaphore_wait(barrier, n_t + n_g - 2)

    def remote(src, dst, send, recv, dev):
        return pltpu.make_async_remote_copy(
            src_ref=src, dst_ref=dst, send_sem=send, recv_sem=recv,
            device_id=dev, device_id_type=MESH,
        )

    def shard_at(base, index):
        return pl.ds(pl.multiple_of(base + index * shard, 64), shard)

    def gather_z(k):
        at = ext.at[shard_at(own, t)]
        return remote(at, at, gz_s.at[k], gz_r.at[k], (g, (t + k) % n_t))

    def landed_z(k):
        at = ext.at[shard_at(own, (t - k + n_t) % n_t)]
        return remote(at, at, gz_s.at[k], gz_r.at[k], (g, (t + k) % n_t))

    def halo(k, up):
        index = (t - k + n_t) % n_t
        src = ext.at[shard_at(own, index)]
        if up:
            return remote(src, ext.at[shard_at(0, index)], gh_s.at[0, k], gh_r.at[0, k], (g + 1, t))
        return remote(src, ext.at[shard_at(2 * own, index)], gh_s.at[1, k], gh_r.at[1, k], (g - 1, t))

    def landed_halo(k, low):
        index = (t - k + n_t) % n_t
        if low:
            at = ext.at[shard_at(0, index)]
            return remote(at, at, gh_s.at[0, k], gh_r.at[0, k], (g - 1, t))
        at = ext.at[shard_at(2 * own, index)]
        return remote(at, at, gh_s.at[1, k], gh_r.at[1, k], (g + 1, t))

    def both(do_up, do_down):
        pl.when(has_high)(do_up)
        pl.when(has_low)(do_down)

    ext[shard_at(own, t), :] = current[...].astype(BF16)
    for k in range(1, n_t):
        gather_z(k).start()
    both(lambda: halo(0, True).start(), lambda: halo(0, False).start())

    @pl.when(jnp.logical_not(has_low))
    def _():
        ext[0:own, :] = jnp.zeros((own, width), BF16)
        halo_in[0] = jnp.zeros((own, width), BF16)

    @pl.when(jnp.logical_not(has_high))
    def _():
        ext[2 * own : 3 * own, :] = jnp.zeros((own, width), BF16)
        halo_in[1] = jnp.zeros((own, width), BF16)

    runs[0] = jnp.zeros((tile, width), F32)
    for k in range(1, n_t):
        landed_z(k).wait_recv()
        both(lambda k=k: halo(k, True).start(), lambda k=k: halo(k, False).start())

    def turn(s, _):
        for c in range(2):
            turned[s, pl.ds(c * tile, tile), :] = tiles[s, c].T
        return 0

    lax.fori_loop(0, slots_n, turn, 0)
    for k in range(n_t):
        both(lambda k=k: landed_halo(k, False).wait_recv(), lambda k=k: landed_halo(k, True).wait_recv())

    for c in range(3 * blocks):
        ext_blocks[c] = ext[pl.ds(c * tile, tile), :]

    def forward(s, _):
        order = plan[s]
        source = ext_blocks[plan[slots_n + s]]
        pair = tiles[order].reshape(2 * tile, tile)
        both_terms = jnp.dot(pair, source, preferred_element_type=F32)
        re, im = both_terms[:tile], both_terms[tile:]
        term = jnp.concatenate(
            [re[:, :half] - im[:, half:], re[:, half:] + im[:, :half]], 1
        )
        runs[s + 1] = term + runs[plan[2 * slots_n + s]]
        return 0

    lax.fori_loop(0, slots_n, forward, 0)
    for r in range(blocks):
        block = runs[plan[3 * slots_n + r]]
        part32[pl.ds(r * tile, tile), :] = block
        part[pl.ds(r * tile, tile), :] = block.astype(BF16)

    def reduce_z(k):
        dest = (t + k) % n_t
        return remote(part.at[shard_at(0, dest)], rs_in.at[k], rs_s.at[k], rs_r.at[k], (g, dest))

    for k in range(1, n_t):
        reduce_z(k).start()
    total = part32[shard_at(0, t), :]
    for k in range(1, n_t):
        reduce_z(k).wait_recv()
        total += rs_in[k].astype(F32)
    z_rows[shard_at(0, t), :] = total.astype(BF16)

    def spread_z(k, landed):
        at = z_rows.at[shard_at(0, (t - k + n_t) % n_t if landed else t)]
        return remote(at, at, ag_s.at[k], ag_r.at[k], (g, (t + k) % n_t))

    for k in range(1, n_t):
        spread_z(k, False).start()
    for k in range(1, n_t):
        spread_z(k, True).wait_recv()

    for r in range(blocks):
        z_blocks[r] = z_rows[pl.ds(r * tile, tile), :]

    base = 3 * slots_n + blocks

    def adjoint(s, _):
        order = plan[base + s]
        source = z_blocks[plan[base + slots_n + s]]
        both_terms = jnp.dot(turned[order], source, preferred_element_type=F32)
        re, im = both_terms[:tile], both_terms[tile:]
        term = jnp.concatenate(
            [re[:, :half] + im[:, half:], re[:, half:] - im[:, :half]], 1
        )
        runs[s + 1] = term + runs[plan[base + 2 * slots_n + s]]
        return 0

    lax.fori_loop(0, slots_n, adjoint, 0)
    for c in list(range(blocks)) + list(range(2 * blocks, 3 * blocks)):
        spread[pl.ds(c * tile, tile), :] = runs[plan[base + 3 * slots_n + c]].astype(BF16)

    def rim(k, up):
        dest = (t + k) % n_t
        src = spread.at[shard_at(2 * own if up else 0, dest)]
        side = 0 if up else 1
        return remote(
            src, halo_in.at[side, shard_at(0, dest)], ah_s.at[side, k], ah_r.at[side, k],
            (g + 1 if up else g - 1, t),
        )

    for k in list(range(1, n_t)) + [0]:
        both(lambda k=k: rim(k, True).start(), lambda k=k: rim(k, False).start())
    for c in range(blocks):
        mid[pl.ds(c * tile, tile), :] = runs[plan[base + 3 * slots_n + blocks + c]]

    def sum_to(k):
        dest = (t + k) % n_t
        return remote(ar_out.at[k], ar_in.at[k], ar_s.at[k], ar_r.at[k], (g, dest))

    for k in list(range(1, n_t)) + [0]:
        both(lambda k=k: rim(k, False).wait_recv(), lambda k=k: rim(k, True).wait_recv())
        at = shard_at(0, (t + k) % n_t)
        total = mid[at, :] + halo_in[0, at, :].astype(F32) + halo_in[1, at, :].astype(F32)
        if k:
            ar_out[k] = total.astype(BF16)
            sum_to(k).start()
    for k in range(1, n_t):
        sum_to(k).wait_recv()
        total += ar_in[k].astype(F32)
    image = total + current[...]
    image_out[...] = image

    def cross(left, right):
        return lax.dot_general(
            left, right, (((0,), (0,)), ((), ())), precision=HIGH, preferred_element_type=F32
        )

    full = cross(image, image)
    gram_mine[0:half, :] = jnp.concatenate(
        [full[:half, :half] + full[half:, half:], full[:half, half:] - full[half:, :half]], 1
    )
    if with_products:
        full = cross(current[...], image)
        gram_mine[half : 2 * half, :] = jnp.concatenate(
            [full[:half, :half] + full[half:, half:], full[:half, half:] - full[half:, :half]], 1
        )
    piece = gram_mine.shape[0] // n_t

    def piece_at(index):
        return pl.ds(pl.multiple_of(index * piece, 8), piece)

    def gram_one(k):
        dest = (t + k) % n_t
        return remote(gram_mine.at[piece_at(dest)], gram_in.at[k], g1_s.at[k], g1_r.at[k], (g, dest))

    for k in range(1, n_t):
        gram_one(k).start()
    total = gram_mine[piece_at(t), :]
    for k in range(1, n_t):
        gram_one(k).wait_recv()
        total += gram_in[k]
    gram_rows[g] = total

    def gram_two(k, landed):
        at = gram_rows.at[(g - k + n_g) % n_g if landed else g]
        return remote(at, at, g2_s.at[k], g2_r.at[k], ((g + k) % n_g, t))

    for k in range(1, n_g):
        gram_two(k, False).start()
    for k in range(1, n_g):
        gram_two(k, True).wait_recv()
    total = gram_rows[0]
    for k in range(1, n_g):
        total += gram_rows[k]
    gram_sum[piece_at(t), :] = total

    def gram_three(k, landed):
        at = gram_sum.at[piece_at((t - k + n_t) % n_t if landed else t)]
        return remote(at, at, g3_s.at[k], g3_r.at[k], (g, (t + k) % n_t))

    for k in range(1, n_t):
        gram_three(k, False).start()
    for k in range(1, n_t):
        gram_three(k, True).wait_recv()
    gram_out[...] = gram_sum[...]

    for k in range(1, n_t):
        gather_z(k).wait_send()
        reduce_z(k).wait_send()
        spread_z(k, False).wait_send()
        sum_to(k).wait_send()
        gram_one(k).wait_send()
        gram_three(k, False).wait_send()
    for k in range(n_t):
        both(lambda k=k: halo(k, True).wait_send(), lambda k=k: halo(k, False).wait_send())
        both(lambda k=k: rim(k, True).wait_send(), lambda k=k: rim(k, False).wait_send())
    for k in range(1, n_g):
        gram_two(k, False).wait_send()


def step(plan, tiles, current, with_products):
    n_g, n_t = lax.axis_size("rows"), lax.axis_size("tiles")
    slots_n, _, tile, _ = tiles.shape
    shard, width = current.shape
    own = shard * n_t
    blocks = own // tile
    rows = width if with_products else width // 2
    dma = pltpu.SemaphoreType.DMA
    vmem = pl.BlockSpec(memory_space=pltpu.VMEM)
    return pl.pallas_call(
        functools.partial(step_kernel, n_g, n_t, with_products, slots_n, blocks),
        out_shape=(
            jax.ShapeDtypeStruct((shard, width), F32),
            jax.ShapeDtypeStruct((rows, width), F32),
        ),
        in_specs=[pl.BlockSpec(memory_space=pltpu.SMEM), vmem, vmem],
        out_specs=(vmem, vmem),
        scratch_shapes=[
            pltpu.VMEM((slots_n, 2 * tile, tile), BF16),
            pltpu.VMEM((3 * own, width), BF16),
            pltpu.VMEM((3 * blocks, tile, width), BF16),
            pltpu.VMEM((blocks, tile, width), BF16),
            pltpu.VMEM((slots_n + 1, tile, width), F32),
            pltpu.VMEM((own, width), F32),
            pltpu.VMEM((own, width), BF16),
            pltpu.VMEM((n_t, shard, width), BF16),
            pltpu.VMEM((own, width), BF16),
            pltpu.VMEM((3 * own, width), BF16),
            pltpu.VMEM((own, width), F32),
            pltpu.VMEM((2, own, width), BF16),
            pltpu.VMEM((n_t, shard, width), BF16),
            pltpu.VMEM((n_t, shard, width), BF16),
            pltpu.VMEM((rows, width), F32),
            pltpu.VMEM((n_t, rows // n_t, width), F32),
            pltpu.VMEM((n_g, rows // n_t, width), F32),
            pltpu.VMEM((rows, width), F32),
            dma((n_t,)), dma((n_t,)), dma((2, n_t)), dma((2, n_t)),
            dma((n_t,)), dma((n_t,)), dma((n_t,)), dma((n_t,)),
            dma((2, n_t)), dma((2, n_t)), dma((n_t,)), dma((n_t,)),
            dma((n_t,)), dma((n_t,)), dma((n_g,)), dma((n_g,)), dma((n_t,)), dma((n_t,)),
        ],
        compiler_params=pltpu.CompilerParams(
            collective_id=1 if with_products else 0,
            has_side_effects=True,
            vmem_limit_bytes=VMEM_BYTES,
        ),
    )(plan, tiles, current)


def whiten_kernel(nodes, gram, image, out, work_r, work_i):
    size = work_r.shape[0]
    work_r[...] = gram[0:size, 0:size]
    work_i[...] = -gram[0:size, size : 2 * size]
    lane = lax.broadcasted_iota(jnp.int32, (size, size), 1)
    sub = lax.broadcasted_iota(jnp.int32, (size, size), 0)
    lane_row = lax.broadcasted_iota(jnp.int32, (1, size), 1)
    sub_col = lax.broadcasted_iota(jnp.int32, (size, 1), 0)

    def eliminate(j, pivots):
        full_r, full_i = work_r[...], work_i[...]
        at = lane == j
        col_r = jnp.sum(jnp.where(at, full_r, 0.0), 1, keepdims=True)
        col_i = jnp.sum(jnp.where(at, full_i, 0.0), 1, keepdims=True)
        row_r = work_r[pl.ds(j, 1), :]
        row_i = work_i[pl.ds(j, 1), :]
        here = lane_row == j
        pivot = jnp.sum(jnp.where(here, row_r, 0.0), 1, keepdims=True)
        inverse = 1.0 / pivot
        below = sub_col > j
        fac_r = jnp.where(below, col_r * inverse, 0.0)
        fac_i = jnp.where(below, col_i * inverse, 0.0)
        row_r = jnp.where(here, 1.0, row_r)
        row_i = jnp.where(here, 0.0, row_i)
        work_r[...] = jnp.where(at, 0.0, full_r) - (fac_r * row_r - fac_i * row_i)
        work_i[...] = jnp.where(at, 0.0, full_i) - (fac_r * row_i + fac_i * row_r)
        return jnp.where(sub_col == j, pivot, pivots)

    pivots = lax.fori_loop(0, size, eliminate, jnp.ones((size, 1), F32))
    scale = math.sqrt(nodes) / jnp.sqrt(pivots)
    low = lane < sub
    inv_r = jnp.where(low, work_r[...], jnp.where(lane == sub, 1.0, 0.0)) * scale
    inv_i = jnp.where(low, work_i[...], 0.0) * scale
    turned = jnp.concatenate(
        [jnp.concatenate([inv_r, -inv_i], 1), jnp.concatenate([inv_i, inv_r], 1)], 0
    )
    out[...] = lax.dot_general(
        image[...], turned, (((1,), (1,)), ((), ())), precision=HIGH, preferred_element_type=F32
    )


def whitened(gram, image, nodes):
    size = image.shape[1] // 2
    vmem = pl.BlockSpec(memory_space=pltpu.VMEM)
    return pl.pallas_call(
        functools.partial(whiten_kernel, nodes),
        out_shape=jax.ShapeDtypeStruct(image.shape, F32),
        in_specs=[vmem, vmem],
        out_specs=vmem,
        scratch_shapes=[pltpu.VMEM((size, size), F32)] * 2,
    )(gram, image)


def on_device(response_tiles, tile_rows, tile_cols, tile_counts, start_block):
    slots = response_tiles[0, 0]
    shard, width = start_block.shape
    columns = width // 2
    tile = slots.shape[-1]
    own = shard * lax.axis_size("tiles")
    blocks = own // tile
    nodes = own * lax.axis_size("rows")
    first_block = lax.axis_index("rows") * blocks - blocks
    live = jnp.arange(slots.shape[0], dtype=jnp.int32) < tile_counts[0, 0]
    row = jnp.clip(tile_rows[0, 0], 0, blocks - 1)
    col = jnp.clip(tile_cols[0, 0] - first_block, 0, 3 * blocks - 1)
    dead = 4 * blocks
    plan = jnp.concatenate(
        [
            ordered(jnp.where(live, row, dead), col, blocks),
            ordered(jnp.where(live, col, dead), row, 3 * blocks),
        ]
    )
    current = start_block.astype(F32)
    image, gram = step(plan, slots, current, False)
    current = whitened(gram, image, nodes)
    image, gram = step(plan, slots, current, True)
    rayleigh = gram[columns:].reshape(columns, 2, columns).swapaxes(0, 1) / nodes
    current = whitened(gram, image, nodes)
    return (current, rayleigh)


def solution(mesh):
    in_specs = (
        P("rows", "tiles", None, None, None, None),
        P("rows", "tiles", None),
        P("rows", "tiles", None),
        P("rows", "tiles"),
        P(("rows", "tiles"), None),
    )
    out_specs = (P(("rows", "tiles"), None), P())
    return jax.shard_map(
        on_device, mesh=mesh, in_specs=in_specs, out_specs=out_specs, check_vma=False
    )
```

time: 963 us -> 201 us (0.21)
  waiting for transfers between devices: 414 us -> 0 us
  Pallas kernels: 0 us -> 186 us
  blocking collectives: 138 us -> 0 us
  other arithmetic: 117 us -> 4.92 us
  matrix products: 91 us -> 0 us
  loops' own time: 76.6 us -> 0 us
  local copies, waits for them, and re-layouts: 73.6 us -> 7.92 us
  starting transfers between devices: 28.4 us -> 0 us
  between operations: 17.3 us -> 1.34 us
    psum x2 -> x0, waiting for transfers between devices: 256 us -> none  [the longest x1 129 us: on_device(): lax.psum((gram_term, inner(current, image)), ('rows', 'tiles'))]
    pallas_call x0 -> x4, Pallas kernels: none -> 186 us  [the longest x2 151 us: step(): pl.pallas_call(functools.partial(step_kernel, n_g, n_t, with_products, sl...]
    psum x2 -> x0, blocking collectives: 113 us -> none  [on_device(): summed = lax.psum(response, 'tiles')]
    another operation x19 -> x0, other arithmetic: 109 us -> none  [the longest x13 68.8 us: whitening(): factor = jnp.linalg.cholesky(paired)]
    dot_general x77 -> x0, matrix products: 88.3 us -> none  [the longest x18 20.5 us: adjoint_visit(): lax.dot_general(pair[1], source, contract, preferred_element_type=jnp.flo...]
    another operation x6 -> x0, loops' own time: 76.6 us -> none  [the longest x2 38.2 us: adjoint_tiles(): lax.fori_loop(0, live_count, adjoint_visit, jnp.zeros((3 * own_rows, widt...]
    reduce_scatter x1 -> x0, waiting for transfers between devices: 59.7 us -> none  [on_device(): lax.psum_scatter(middle + from_below + from_above, 'tiles', scatter_dimen...]
    unnamed x5 -> x0, waiting for transfers between devices: 56.9 us -> none
  transfers between devices with their start and end apart: 12 -> 0, of which waited for: 10 -> 0; matrix products, arithmetic and copies ran while one was open for 0% -> 0% of each run, Pallas kernels for 0% -> 0%
where the time goes in v1:
time: 201 us; the launch traced here: 200 us
  Pallas kernels  186 us (93%)
  local copies, waits for them, and re-layouts  7.92 us (4%)
  other arithmetic  4.92 us (2%)
    pallas_call x2, Pallas kernels, step(): pl.pallas_call(functools.partial(step_kernel, n_g, n_t, with_products, sl...  151 us
    pallas_call x2, Pallas kernels, whitened(): pl.pallas_call(functools.partial(whiten_kernel, nodes), out_shape=jax.Sha...  35.1 us
    unnamed x14, local copies, waits for them, and re-layouts  7.84 us

profile of v1, /device:TPU:11, one launch (start us, length us, event | category | flops | bytes accessed | tf_op | source)
XLA Modules:
  0.0 200.4 jit_solution(8344115707239473972)
XLA Ops:
  1.3 0.7 clamp_bitcast_fusion.1
  1.9 0.7 compare_select_fusion
  2.6 0.1 convert_reduce_fusion.1
  2.7 0.1 select_reduce_fusion
  2.8 0.1 fusion.4
  2.9 0.1 slice_compare_fusion
  3.0 0.1 convert_reduce_fusion
  3.1 0.1 fusion.7
  3.1 0.1 convert_reduce_fusion.2
  3.2 0.1 select_reduce_fusion.3
  3.3 0.1 fusion.5
  3.4 0.1 slice_compare_fusion.1
  3.5 0.1 convert_reduce_fusion.3
  3.6 0.1 fusion.6
  3.7 0.1 concatenate.11.plan
  3.8 0.9 convert_element_type.21.current
  4.7 0.0 copy-start
  4.7 2.1 %copy-done = bf16[1,1,15,2,256,256]{5,4,3,2,1,0:T(8,128)(2,1)S(1)} copy-done((bf16[1,1,15,2,256,256]{5,4,3,2,1,0:T(8,128)(2,1)S(1)}, bf16[1,1,15,2,256,256]{5,4,3,2,1,0:T(8,128)(2,1)}, u32[]{:S(2)}) %copy-start) | copy-done | bytes 3932184
  6.8 72.1 %shard_map.68 = (f32[192,256]{1,0:T(8,128)S(1)}, f32[128,256]{1,0:T(8,128)S(1)}) custom-call(s32[102]{0:T(128)S(1)} %concatenate.11.plan, bf16[15,2,256,256]{3,2,1,0:T(8,128)(2,1)S(1)} %bitcast.17, f32[192,256]{1,0:T(8,128)S(1)} %convert_element_type.21.current), custom_call_target="tpu_custom_call" | custom-call | tf_op jit(solution)/shard_map/pallas_call | solution.py:297
  79.0 0.0 copy-start.5
  79.0 0.7 copy-done.5
  79.7 0.0 copy-start.6
  79.7 0.7 copy-done.6
  80.3 17.5 %shard_map.69.current = f32[192,256]{1,0:T(8,128)} custom-call(f32[128,256]{1,0:T(8,128)} %copy-done.6, f32[192,256]{1,0:T(8,128)} %copy-done.5), custom_call_target="tpu_custom_call" | custom-call | tf_op jit(solution)/shard_map/pallas_call | solution.py:381
  97.9 2.1 %copy-done.1 = bf16[1,1,15,2,256,256]{5,4,3,2,1,0:T(8,128)(2,1)S(1)} copy-done((bf16[1,1,15,2,256,256]{5,4,3,2,1,0:T(8,128)(2,1)S(1)}, bf16[1,1,15,2,256,256]{5,4,3,2,1,0:T(8,128)(2,1)}, u32[]{:S(2)}) %copy-start.1) | copy-done | bytes 3932184
  100.0 0.9 copy-done.2
  100.9 79.0 %shard_map.70 = (f32[192,256]{1,0:T(8,128)S(1)}, f32[256,256]{1,0:T(8,128)S(1)}) custom-call(s32[102]{0:T(128)S(1)} %concatenate.11.plan, bf16[15,2,256,256]{3,2,1,0:T(8,128)(2,1)S(1)} %bitcast.18, f32[192,256]{1,0:T(8,128)S(1)} %copy-done.2), custom_call_target="tpu_custom_call" | custom-call | tf_op jit(solution)/shard_map/pallas_call | solution.py:297
  179.9 0.0 copy-start.3
  179.9 0.7 copy-done.3
  180.6 0.7 copy-done.4
  181.3 17.6 %shard_map.71 = f32[192,256]{1,0:T(8,128)} custom-call(f32[256,256]{1,0:T(8,128)} %copy-done.3, f32[192,256]{1,0:T(8,128)} %copy-done.4), custom_call_target="tpu_custom_call" | custom-call | tf_op jit(solution)/shard_map/pallas_call | solution.py:381
  198.8 1.6 bitcast_bitcast_fusion
  (5 shorter events, 0.0 us)
Async XLA Ops:
  4.7 2.1 %copy-start = (bf16[1,1,15,2,256,256]{5,4,3,2,1,0:T(8,128)(2,1)S(1)}, bf16[1,1,15,2,256,256]{5,4,3,2,1,0:T(8,128)(2,1)}, u32[]{:S(2)}) copy-start(bf16[1,1,15,2,256,256]{5,4,3,2,1,0:T(8,128)(2,1)} %param.5) | copy-start | bytes 11796484
  79.0 0.7 copy-start.5
  79.7 0.7 copy-start.6
  97.9 2.1 %copy-start.1 = (bf16[1,1,15,2,256,256]{5,4,3,2,1,0:T(8,128)(2,1)S(1)}, bf16[1,1,15,2,256,256]{5,4,3,2,1,0:T(8,128)(2,1)}, u32[]{:S(2)}) copy-start(bf16[1,1,15,2,256,256]{5,4,3,2,1,0:T(8,128)(2,1)} %param.5) | copy-start | bytes 11796484
  100.0 0.9 copy-start.2
  179.9 0.7 copy-start.3
  180.6 0.7 copy-start.4

commit v2 on v0

v2 whole, which is shorter than its diff:
```python
import functools
import math

import jax
import jax.numpy as jnp
from jax import lax
from jax.experimental import pallas as pl
from jax.experimental.pallas import tpu as pltpu
from jax.sharding import PartitionSpec as P

HIGH = lax.Precision.HIGHEST
MESH = pl.DeviceIdType.MESH
VMEM_BYTES = 48 * 1024 * 1024
F32 = jnp.float32
BF16 = jnp.bfloat16
ITERS = 2


def ordered(key, other, outs):
    count = key.shape[0]
    slot = jnp.arange(count, dtype=jnp.int32)
    before = (key[:, None] < key[None, :]) | (
        (key[:, None] == key[None, :]) & (slot[:, None] < slot[None, :])
    )
    rank = jnp.sum(before.astype(jnp.int32), 0)
    hot = (rank[:, None] == slot[None, :]).astype(jnp.int32)
    order = jnp.sum(hot * slot[:, None], 0)
    target = jnp.sum(hot * key[:, None], 0)
    source = jnp.sum(hot * other[:, None], 0)
    same = jnp.concatenate([jnp.zeros((1,), bool), target[1:] == target[:-1]])
    previous = jnp.where(same, slot, 0)
    out = jnp.arange(outs, dtype=jnp.int32)
    upto = jnp.sum((target[:, None] <= out[None, :]).astype(jnp.int32), 0)
    present = jnp.any(target[:, None] == out[None, :], 0)
    return jnp.concatenate([order, source, previous, jnp.where(present, upto, 0)])


def whitening(gram, work_r, work_i, nodes):
    size = work_r.shape[0]
    work_r[...] = gram[:, 0:size]
    work_i[...] = -gram[:, size : 2 * size]
    lane = lax.broadcasted_iota(jnp.int32, (size, size), 1)
    sub = lax.broadcasted_iota(jnp.int32, (size, size), 0)
    lane_row = lax.broadcasted_iota(jnp.int32, (1, size), 1)
    sub_col = lax.broadcasted_iota(jnp.int32, (size, 1), 0)

    def eliminate(j, pivots):
        full_r, full_i = work_r[...], work_i[...]
        at = lane == j
        col_r = jnp.sum(jnp.where(at, full_r, 0.0), 1, keepdims=True)
        col_i = jnp.sum(jnp.where(at, full_i, 0.0), 1, keepdims=True)
        row_r = work_r[pl.ds(j, 1), :]
        row_i = work_i[pl.ds(j, 1), :]
        here = lane_row == j
        pivot = jnp.sum(jnp.where(here, row_r, 0.0), 1, keepdims=True)
        inverse = 1.0 / pivot
        below = sub_col > j
        fac_r = jnp.where(below, col_r * inverse, 0.0)
        fac_i = jnp.where(below, col_i * inverse, 0.0)
        row_r = jnp.where(here, 1.0, row_r)
        row_i = jnp.where(here, 0.0, row_i)
        work_r[...] = jnp.where(at, 0.0, full_r) - (fac_r * row_r - fac_i * row_i)
        work_i[...] = jnp.where(at, 0.0, full_i) - (fac_r * row_i + fac_i * row_r)
        return jnp.where(sub_col == j, pivot, pivots)

    pivots = lax.fori_loop(0, size, eliminate, jnp.ones((size, 1), F32))
    scale = math.sqrt(nodes) / jnp.sqrt(pivots)
    low = lane < sub
    inv_r = jnp.where(low, work_r[...], jnp.where(lane == sub, 1.0, 0.0)) * scale
    inv_i = jnp.where(low, work_i[...], 0.0) * scale
    return jnp.concatenate(
        [jnp.concatenate([inv_r, -inv_i], 1), jnp.concatenate([inv_i, inv_r], 1)], 0
    )


def kernel(
    n_g, n_t, slots_n, blocks,
    plan, tiles, start, subspace_out, rayleigh_out,
    turned, cur, ext, wide, ext_blocks, z_blocks, runs, part, rs_in, z_own, z_in, z_rows,
    spread, mid, halo_in, ar_out, ar_in,
    gram_mine, gram_in, gram_rows, gram_sum, work_r, work_i, white,
    gz_s, gz_r, gh_s, gh_r, rs_s, rs_r, ag_s, ag_r, ah_s, ah_r, ar_s, ar_r,
    g1_s, g1_r, g2_s, g2_r, g3_s, g3_r,
):
    g = lax.axis_index("rows")
    t = lax.axis_index("tiles")
    has_low = g > 0
    has_high = g < n_g - 1
    tile = tiles.shape[-1]
    shard, width = start.shape
    half = width // 2
    own = shard * n_t
    nodes = own * n_g
    base = 3 * slots_n + blocks

    barrier = pltpu.get_barrier_semaphore()
    for k in range(1, n_t):
        pl.semaphore_signal(barrier, inc=1, device_id=(g, (t + k) % n_t), device_id_type=MESH)

    for k in range(1, n_g):
        pl.semaphore_signal(barrier, inc=1, device_id=((g + k) % n_g, t), device_id_type=MESH)
    pl.semaphore_wait(barrier, n_t + n_g - 2)

    def remote(src, dst, send, recv, dev):
        return pltpu.make_async_remote_copy(
            src_ref=src, dst_ref=dst, send_sem=send, recv_sem=recv,
            device_id=dev, device_id_type=MESH,
        )

    def shard_at(base, index):
        return pl.ds(pl.multiple_of(base + index * shard, 64), shard)

    def both(do_up, do_down):
        pl.when(has_high)(do_up)
        pl.when(has_low)(do_down)

    def cross(left, right):
        full = lax.dot_general(
            left, right, (((0,), (0,)), ((), ())), precision=HIGH, preferred_element_type=F32
        )
        return jnp.concatenate(
            [full[:half, :half] + full[half:, half:], full[:half, half:] - full[half:, :half]], 1
        )

    def gathering(it, buf):
        def along(k, landed):
            at = buf.at[shard_at(own, (t - k + n_t) % n_t if landed else t)]
            return remote(at, at, gz_s.at[it, k], gz_r.at[it, k], (g, (t + k) % n_t))

        def halo(k, up):
            index = (t - k + n_t) % n_t
            side = 0 if up else 1
            return remote(
                buf.at[shard_at(own, index)],
                buf.at[shard_at(0 if up else 2 * own, index)],
                gh_s.at[it, side, k], gh_r.at[it, side, k],
                (g + 1 if up else g - 1, t),
            )

        def landed_halo(k, low):
            index = (t - k + n_t) % n_t
            side = 0 if low else 1
            at = buf.at[shard_at(0 if low else 2 * own, index)]
            return remote(
                at, at, gh_s.at[it, side, k], gh_r.at[it, side, k],
                (g - 1 if low else g + 1, t),
            )

        def begin(rows):
            buf[shard_at(own, t), :] = rows
            for k in range(1, n_t):
                along(k, False).start()
            both(lambda: halo(0, True).start(), lambda: halo(0, False).start())

        def forward_halo():
            for k in range(1, n_t):
                along(k, True).wait_recv()
                both(lambda k=k: halo(k, True).start(), lambda k=k: halo(k, False).start())

        def finish():
            for k in range(n_t):
                both(
                    lambda k=k: landed_halo(k, False).wait_recv(),
                    lambda k=k: landed_halo(k, True).wait_recv(),
                )
            for k in range(1, n_t):
                along(k, False).wait_send()
            for k in range(n_t):
                both(lambda k=k: halo(k, True).wait_send(), lambda k=k: halo(k, False).wait_send())

        return begin, forward_halo, finish

    cur[...] = start[...].astype(F32)
    begin, forward_halo, finish = gathering(0, ext)
    begin(start[...])

    @pl.when(jnp.logical_not(has_low))
    def _():
        ext[0:own, :] = jnp.zeros((own, width), BF16)
        wide[0:own, :] = jnp.zeros((own, width), F32)
        for it in range(ITERS):
            halo_in[it, 0] = jnp.zeros((own, width), BF16)

    @pl.when(jnp.logical_not(has_high))
    def _():
        ext[2 * own : 3 * own, :] = jnp.zeros((own, width), BF16)
        wide[2 * own : 3 * own, :] = jnp.zeros((own, width), F32)
        for it in range(ITERS):
            halo_in[it, 1] = jnp.zeros((own, width), BF16)

    runs[0] = jnp.zeros((tile, width), F32)
    forward_halo()

    def turn(s, _):
        for c in range(2):
            turned[s, pl.ds(c * tile, tile), :] = tiles[s, c].T
        return 0

    lax.fori_loop(0, slots_n, turn, 0)
    finish()
    for c in range(3 * blocks):
        ext_blocks[c] = ext[pl.ds(c * tile, tile), :]

    for it in range(ITERS):
        last = it == ITERS - 1

        def forward(s, _):
            pair = tiles[plan[s]].reshape(2 * tile, tile)
            both_terms = jnp.dot(pair, ext_blocks[plan[slots_n + s]], preferred_element_type=F32)
            re, im = both_terms[:tile], both_terms[tile:]
            term = jnp.concatenate(
                [re[:, :half] - im[:, half:], re[:, half:] + im[:, :half]], 1
            )
            runs[s + 1] = term + runs[plan[2 * slots_n + s]]
            return 0

        lax.fori_loop(0, slots_n, forward, 0)
        for r in range(blocks):
            part[pl.ds(r * tile, tile), :] = runs[plan[3 * slots_n + r]]

        def reduce_z(k):
            dest = (t + k) % n_t
            return remote(
                part.at[shard_at(0, dest)], rs_in.at[it, k], rs_s.at[it, k], rs_r.at[it, k], (g, dest)
            )

        for k in range(1, n_t):
            reduce_z(k).start()
        total = part[shard_at(0, t), :]
        for k in range(1, n_t):
            reduce_z(k).wait_recv()
            total += rs_in[it, k]
        z_own[...] = total.astype(BF16)

        def spread_z(k):
            return remote(z_own, z_in.at[it, k], ag_s.at[it, k], ag_r.at[it, k], (g, (t + k) % n_t))

        for k in range(1, n_t):
            spread_z(k).start()
        z_rows[shard_at(0, t), :] = z_own[...]
        for k in range(1, n_t):
            spread_z(k).wait_recv()
            z_rows[shard_at(0, (t - k + n_t) % n_t), :] = z_in[it, k]
        for r in range(blocks):
            z_blocks[r] = z_rows[pl.ds(r * tile, tile), :]

        def adjoint(s, _):
            source = z_blocks[plan[base + slots_n + s]]
            both_terms = jnp.dot(turned[plan[base + s]], source, preferred_element_type=F32)
            re, im = both_terms[:tile], both_terms[tile:]
            term = jnp.concatenate(
                [re[:, :half] + im[:, half:], re[:, half:] - im[:, :half]], 1
            )
            runs[s + 1] = term + runs[plan[base + 2 * slots_n + s]]
            return 0

        lax.fori_loop(0, slots_n, adjoint, 0)
        for c in list(range(blocks)) + list(range(2 * blocks, 3 * blocks)):
            spread[pl.ds(c * tile, tile), :] = runs[plan[base + 3 * slots_n + c]].astype(BF16)

        def rim(k, up):
            dest = (t + k) % n_t
            side = 0 if up else 1
            return remote(
                spread.at[shard_at(2 * own if up else 0, dest)],
                halo_in.at[it, side, shard_at(0, dest)],
                ah_s.at[it, side, k], ah_r.at[it, side, k],
                (g + 1 if up else g - 1, t),
            )

        for k in list(range(1, n_t)) + [0]:
            both(lambda k=k: rim(k, True).start(), lambda k=k: rim(k, False).start())
        for c in range(blocks):
            mid[pl.ds(c * tile, tile), :] = runs[plan[base + 3 * slots_n + blocks + c]]

        def sum_to(k):
            return remote(
                ar_out.at[k], ar_in.at[it, k], ar_s.at[it, k], ar_r.at[it, k], (g, (t + k) % n_t)
            )

        for k in list(range(1, n_t)) + [0]:
            both(lambda k=k: rim(k, False).wait_recv(), lambda k=k: rim(k, True).wait_recv())
            at = shard_at(0, (t + k) % n_t)
            total = mid[at, :] + halo_in[it, 0, at, :].astype(F32) + halo_in[it, 1, at, :].astype(F32)
            if k:
                ar_out[k] = total.astype(BF16)
                sum_to(k).start()
        for k in range(1, n_t):
            sum_to(k).wait_recv()
            total += ar_in[it, k].astype(F32)
        image = total + cur[...]
        if not last:
            begin, forward_halo, finish = gathering(1, wide)
            begin(image)

        gram_mine[it, 0:half, :] = cross(image, image)
        if last:
            gram_mine[it, half : 2 * half, :] = cross(cur[...], image)
        cur[...] = image
        piece = (2 * half if last else half) // n_t

        def piece_at(index):
            return pl.ds(pl.multiple_of(index * piece, 8), piece)

        def gram_one(k):
            dest = (t + k) % n_t
            return remote(
                gram_mine.at[it, piece_at(dest)], gram_in.at[it, k, pl.ds(0, piece)],
                g1_s.at[it, k], g1_r.at[it, k], (g, dest),
            )

        for k in range(1, n_t):
            gram_one(k).start()
        total = gram_mine[it, piece_at(t), :]
        for k in range(1, n_t):
            gram_one(k).wait_recv()
            total += gram_in[it, k, 0:piece, :]
        gram_rows[it, g, 0:piece, :] = total

        def gram_two(k, landed):
            at = gram_rows.at[it, (g - k + n_g) % n_g if landed else g, pl.ds(0, piece)]
            return remote(at, at, g2_s.at[it, k], g2_r.at[it, k], ((g + k) % n_g, t))

        for k in range(1, n_g):
            gram_two(k, False).start()
        for k in range(1, n_g):
            gram_two(k, True).wait_recv()
        total = gram_rows[it, 0, 0:piece, :]
        for k in range(1, n_g):
            total += gram_rows[it, k, 0:piece, :]
        gram_sum[it, piece_at(t), :] = total

        def gram_three(k, landed):
            at = gram_sum.at[it, piece_at((t - k + n_t) % n_t if landed else t)]
            return remote(at, at, g3_s.at[it, k], g3_r.at[it, k], (g, (t + k) % n_t))

        for k in range(1, n_t):
            gram_three(k, False).start()
        for k in range(1, n_t):
            gram_three(k, True).wait_recv()

        for k in range(1, n_t):
            reduce_z(k).wait_send()
            spread_z(k).wait_send()
            sum_to(k).wait_send()
            gram_one(k).wait_send()
            gram_three(k, False).wait_send()
        for k in range(n_t):
            both(lambda k=k: rim(k, True).wait_send(), lambda k=k: rim(k, False).wait_send())
        for k in range(1, n_g):
            gram_two(k, False).wait_send()

        if not last:
            forward_halo()
        white[...] = whitening(gram_sum[it, 0:half, :], work_r, work_i, nodes).T

        def times_white(rows):
            return jnp.dot(rows, white[...], precision=HIGH, preferred_element_type=F32)

        if last:
            subspace_out[...] = times_white(cur[...])
            products = gram_sum[it, half : 2 * half, :]
            rayleigh_out[0] = products[:, :half] / nodes
            rayleigh_out[1] = products[:, half:] / nodes
        else:
            cur[...] = times_white(cur[...])
            finish()

            def narrow(c, _):
                rows = wide[pl.ds(pl.multiple_of(c * tile, tile), tile), :]
                ext_blocks[c] = times_white(rows).astype(BF16)
                return 0

            lax.fori_loop(0, 3 * blocks, narrow, 0)


def iterate(plan, tiles, start):
    n_g, n_t = lax.axis_size("rows"), lax.axis_size("tiles")
    slots_n, _, tile, _ = tiles.shape
    shard, width = start.shape
    half = width // 2
    own = shard * n_t
    blocks = own // tile
    vmem = pl.BlockSpec(memory_space=pltpu.VMEM)
    along = pltpu.SemaphoreType.DMA((ITERS, n_t))
    sides = pltpu.SemaphoreType.DMA((ITERS, 2, n_t))
    groups = pltpu.SemaphoreType.DMA((ITERS, n_g))
    scratch = [
        ((slots_n, 2 * tile, tile), BF16),
        ((shard, width), F32),
        ((3 * own, width), BF16),
        ((3 * own, width), F32),
        ((3 * blocks, tile, width), BF16),
        ((blocks, tile, width), BF16),
        ((slots_n + 1, tile, width), F32),
        ((own, width), F32),
        ((ITERS, n_t, shard, width), F32),
        ((shard, width), BF16),
        ((ITERS, n_t, shard, width), BF16),
        ((own, width), BF16),
        ((3 * own, width), BF16),
        ((own, width), F32),
        ((ITERS, 2, own, width), BF16),
        ((n_t, shard, width), BF16),
        ((ITERS, n_t, shard, width), BF16),
        ((ITERS, width, width), F32),
        ((ITERS, n_t, width // n_t, width), F32),
        ((ITERS, n_g, width // n_t, width), F32),
        ((ITERS, width, width), F32),
        ((half, half), F32),
        ((half, half), F32),
        ((width, width), F32),
    ]
    return pl.pallas_call(
        functools.partial(kernel, n_g, n_t, slots_n, blocks),
        out_shape=(
            jax.ShapeDtypeStruct((shard, width), F32),
            jax.ShapeDtypeStruct((2, half, half), F32),
        ),
        in_specs=[pl.BlockSpec(memory_space=pltpu.SMEM), vmem, vmem],
        out_specs=(vmem, vmem),
        scratch_shapes=[pltpu.VMEM(shape, dtype) for shape, dtype in scratch]
        + [along, along, sides, sides, along, along, along, along, sides, sides, along, along]
        + [along, along, groups, groups, along, along],
        compiler_params=pltpu.CompilerParams(
            collective_id=0, has_side_effects=True, vmem_limit_bytes=VMEM_BYTES
        ),
    )(plan, tiles, start)


def on_device(response_tiles, tile_rows, tile_cols, tile_counts, start_block):
    slots = response_tiles[0, 0]
    shard = start_block.shape[0]
    tile = slots.shape[-1]
    own = shard * lax.axis_size("tiles")
    blocks = own // tile
    first_block = lax.axis_index("rows") * blocks - blocks
    live = jnp.arange(slots.shape[0], dtype=jnp.int32) < tile_counts[0, 0]
    row = jnp.clip(tile_rows[0, 0], 0, blocks - 1)
    col = jnp.clip(tile_cols[0, 0] - first_block, 0, 3 * blocks - 1)
    dead = 4 * blocks
    plan = jnp.concatenate(
        [
            ordered(jnp.where(live, row, dead), col, blocks),
            ordered(jnp.where(live, col, dead), row, 3 * blocks),
        ]
    )
    return iterate(plan, slots, start_block)


def solution(mesh):
    in_specs = (
        P("rows", "tiles", None, None, None, None),
        P("rows", "tiles", None),
        P("rows", "tiles", None),
        P("rows", "tiles"),
        P(("rows", "tiles"), None),
    )
    out_specs = (P(("rows", "tiles"), None), P())
    return jax.shard_map(
        on_device, mesh=mesh, in_specs=in_specs, out_specs=out_specs, check_vma=False
    )
```

time: 963 us -> 210 us (0.22)
  waiting for transfers between devices: 414 us -> 0 us
  Pallas kernels: 0 us -> 202 us
  blocking collectives: 138 us -> 0 us
  other arithmetic: 117 us -> 2.43 us
  matrix products: 91 us -> 0 us
  loops' own time: 76.6 us -> 0 us
  local copies, waits for them, and re-layouts: 73.6 us -> 4.43 us
  starting transfers between devices: 28.4 us -> 0 us
  between operations: 17.3 us -> 1.3 us
    psum x2 -> x0, waiting for transfers between devices: 256 us -> none  [the longest x1 129 us: on_device(): lax.psum((gram_term, inner(current, image)), ('rows', 'tiles'))]
    pallas_call x0 -> x1, Pallas kernels: none -> 202 us  [iterate(): pl.pallas_call(functools.partial(kernel, n_g, n_t, slots_n, blocks), out_...]
    psum x2 -> x0, blocking collectives: 113 us -> none  [on_device(): summed = lax.psum(response, 'tiles')]
    another operation x19 -> x0, other arithmetic: 109 us -> none  [the longest x13 68.8 us: whitening(): factor = jnp.linalg.cholesky(paired)]
    dot_general x77 -> x0, matrix products: 88.3 us -> none  [the longest x18 20.5 us: adjoint_visit(): lax.dot_general(pair[1], source, contract, preferred_element_type=jnp.flo...]
    another operation x6 -> x0, loops' own time: 76.6 us -> none  [the longest x2 38.2 us: adjoint_tiles(): lax.fori_loop(0, live_count, adjoint_visit, jnp.zeros((3 * own_rows, widt...]
    reduce_scatter x1 -> x0, waiting for transfers between devices: 59.7 us -> none  [on_device(): lax.psum_scatter(middle + from_below + from_above, 'tiles', scatter_dimen...]
    unnamed x5 -> x0, waiting for transfers between devices: 56.9 us -> none
  transfers between devices with their start and end apart: 12 -> 0, of which waited for: 10 -> 0; matrix products, arithmetic and copies ran while one was open for 0% -> 0% of each run, Pallas kernels for 0% -> 0%
where the time goes in v2:
time: 210 us
  Pallas kernels  202 us (96%)
  local copies, waits for them, and re-layouts  4.43 us (2%)
  other arithmetic  2.43 us (1%)
    pallas_call x1, Pallas kernels, iterate(): pl.pallas_call(functools.partial(kernel, n_g, n_t, slots_n, blocks), out_...  202 us
    unnamed x6, local copies, waits for them, and re-layouts  4.35 us

profile of v2, /device:TPU:11, one launch (start us, length us, event | category | flops | bytes accessed | tf_op | source)
XLA Modules:
  0.0 210.3 jit_solution(16881065458058425659)
XLA Ops:
  1.3 0.7 clamp_bitcast_fusion.1
  1.9 0.7 compare_select_fusion
  2.6 0.1 convert_reduce_fusion.1
  2.7 0.1 select_reduce_fusion
  2.8 0.1 fusion.4
  2.9 0.1 slice_compare_fusion
  3.0 0.1 convert_reduce_fusion
  3.1 0.1 fusion.7
  3.1 0.1 convert_reduce_fusion.2
  3.2 0.1 select_reduce_fusion.3
  3.3 0.1 fusion.5
  3.4 0.1 slice_compare_fusion.1
  3.5 0.1 convert_reduce_fusion.3
  3.6 0.1 fusion.6
  3.7 0.1 concatenate.11.plan
  3.8 0.0 copy-start
  3.8 2.1 %copy-done = bf16[1,1,15,2,256,256]{5,4,3,2,1,0:T(8,128)(2,1)S(1)} copy-done((bf16[1,1,15,2,256,256]{5,4,3,2,1,0:T(8,128)(2,1)S(1)}, bf16[1,1,15,2,256,256]{5,4,3,2,1,0:T(8,128)(2,1)}, u32[]{:S(2)}) %copy-start) | copy-done | bytes 3932184
  5.9 0.0 copy-start.1
  5.9 0.9 copy-done.1
  6.8 202.1 %shard_map.68 = (f32[192,256]{1,0:T(8,128)S(1)}, f32[2,128,128]{2,1,0:T(8,128)S(1)}) custom-call(s32[102]{0:T(128)S(1)} %concatenate.11.plan, bf16[15,2,256,256]{3,2,1,0:T(8,128)(2,1)S(1)} %bitcast.10, bf16[192,256]{1,0:T(8,128)(2,1)S(1)} %copy-done.1), custom_call_target="tpu_custom_call" | custom-call | tf_op jit(solution)/shard_map/pallas_call | solution.py:414
  208.9 0.7 copy.10
  209.6 0.7 copy.11
  (2 shorter events, 0.0 us)
Async XLA Ops:
  3.8 2.1 %copy-start = (bf16[1,1,15,2,256,256]{5,4,3,2,1,0:T(8,128)(2,1)S(1)}, bf16[1,1,15,2,256,256]{5,4,3,2,1,0:T(8,128)(2,1)}, u32[]{:S(2)}) copy-start(bf16[1,1,15,2,256,256]{5,4,3,2,1,0:T(8,128)(2,1)} %param.5) | copy-start | bytes 11796484
  5.9 0.9 copy-start.1
